TPU v7x, 32 devices: a whole 2x2x4 slice. The times are simulated.
32 devices in a mesh: rep: 2 (over y), seq: 4 (over z), head: 4 (over x, core).
Axes of the slice: x: 2, y: 2, z: 4, core: 2. Of those that a mesh axis runs over, the one named last changes fastest.
Arguments:
- queries: bfloat16 [4096, 1024], P(('rep', 'seq', 'head')), parts along dimension 0, may hold values from -6 to 6
- keys: bfloat16 [4096, 2, 1024], P(('rep', 'seq', 'head')), parts along dimension 0, may hold values from -6 to 6
- values: bfloat16 [4096, 2, 1024], P(('rep', 'seq', 'head')), parts along dimension 0, may hold values from -6 to 6
- out_gate: bfloat16 [4096, 1024], P(('rep', 'seq', 'head')), parts along dimension 0, may hold values from -6 to 6
- write_rate: bfloat16 [4096, 2, 8], P(('rep', 'seq', 'head')), parts along dimension 0, may hold values from 0 to 2
- log_decay: bfloat16 [4096, 8], P(('rep', 'seq', 'head')), parts along dimension 0, may hold values from -0.7 to 0
- doc_starts: int32 [8], P('rep'), parts along dimension 0, may hold values from 0 to 2047, as said below
- norm_gain: float32 [128], replicated, may hold values from 0.1 to 1.9
- out_weight: bfloat16 [1024, 2048], P(None, 'head'), may hold values from -0.1875 to 0.1875
Outputs:
- layer_out: bfloat16 [4096, 2048], P(('rep', 'seq'), 'head'), parts along dimension 0
There are 2 independent parts, one for each index of `rep`. A program takes and returns all parts, laid end to end along the dimension named above; an argument that names none is the same for every part. Nothing has to cross between parts.
Inputs may be any that keep to these rules, and one draw needn't show every extreme that they name: `doc_starts`: rises strictly from 0; one document holds exactly 1024 tokens, every other fewer, each at least one.
All inputs are finite; a program needn't handle non-finite values.
Results may differ from a plain program's by a relative error of at most 0.007.
Values may be sent and summed in bfloat16 or wider, within the bound.
A program may use at most 64 MiB of HBM per device.

v0:
```python
import math
import jax
import jax.numpy as jnp
from jax import lax
from jax.sharding import PartitionSpec as P

PRECISE_SETTING = lax.Precision.HIGHEST


def passed_along(value, axis, steps):
    count = lax.axis_size(axis)
    initial, last = (max(0, -steps), min(count, count - steps))
    return lax.ppermute(value, axis, [(source, source + steps) for source in range(initial, last)])


def doc_index(token_position, doc_starts):
    return jnp.sum((token_position[:, None] >= doc_starts[None, :]).astype(jnp.int32), 1) - 1


def advance(carry_pair, step_pair):
    current_state, through_map = carry_pair
    step_map, step_add = step_pair
    new_state = (
        jnp.einsum("hde,hef->hdf", step_map, current_state, precision=PRECISE_SETTING) + step_add
    )
    new_map = jnp.einsum("hde,hef->hdf", step_map, through_map, precision=PRECISE_SETTING)
    return ((new_state, new_map), (current_state, through_map))


def stretch_pieces(
    query_part,
    key_part,
    value_part,
    rate_part,
    decay_part,
    first_pos,
    doc_starts,
    heads_here,
    head_depth,
):
    group_len = query_part.shape[0]
    steps_len = 2 * group_len
    block_len = math.gcd(128, steps_len)
    block_count = steps_len // block_len
    half_len = block_len // 2
    read_rows = (
        query_part.reshape(group_len, heads_here, head_depth).astype(jnp.float32).transpose(1, 0, 2)
    )
    read_rows = read_rows.reshape(heads_here, block_count, half_len, head_depth)
    key_rows = key_part.reshape(group_len, 2, heads_here, head_depth).astype(jnp.float32)
    key_rows = key_rows / jnp.sqrt(jnp.sum(key_rows * key_rows, -1, keepdims=True) + 1e-06)
    key_rows = key_rows.transpose(2, 0, 1, 3).reshape(
        heads_here, block_count, block_len, head_depth
    )
    value_rows = value_part.reshape(group_len, 2, heads_here, head_depth).astype(jnp.float32)
    value_rows = value_rows.transpose(2, 0, 1, 3).reshape(
        heads_here, block_count, block_len, head_depth
    )
    rate_rows = (
        rate_part.astype(jnp.float32).transpose(2, 0, 1).reshape(heads_here, block_count, block_len)
    )
    decay_logs = decay_part.reshape(group_len, heads_here).astype(jnp.float32)
    decay_logs = jnp.stack([decay_logs, jnp.zeros_like(decay_logs)], 1).transpose(2, 0, 1)
    totals = jnp.cumsum(decay_logs.reshape(heads_here, block_count, block_len), -1)
    doc_ids = doc_index(first_pos + jnp.arange(group_len, dtype=jnp.int32), doc_starts)
    doc_before = doc_index(jnp.reshape(first_pos - 1, (1,)), doc_starts)
    step_docs = jnp.repeat(doc_ids, 2).reshape(block_count, block_len)
    prior_docs = jnp.concatenate([doc_before, step_docs[:-1, -1]])
    step_index = jnp.arange(block_len)
    within = step_index[:, None] >= step_index[None, :]
    strict = step_index[:, None] > step_index[None, :]
    same_doc = step_docs[:, :, None] == step_docs[:, None, :]
    causal_doc = within & same_doc
    spread = totals[..., :, None] - totals[..., None, :]
    decay_ratio = jnp.where(causal_doc, jnp.exp(jnp.where(causal_doc, spread, 0.0)), 0.0)
    start_gain = jnp.where(step_docs == prior_docs[:, None], jnp.exp(totals), 0.0)
    end_gain = jnp.where(step_docs == step_docs[:, -1:], jnp.exp(totals[..., -1:] - totals), 0.0)
    key_gram = jnp.einsum("hcid,hcjd->hcij", key_rows, key_rows, precision=PRECISE_SETTING)
    lower_part = jnp.where(strict, rate_rows[..., :, None] * decay_ratio * key_gram, 0.0)
    system = lower_part + jnp.eye(block_len, dtype=jnp.float32)
    right_side = jnp.concatenate(
        [rate_rows[..., None] * value_rows, (rate_rows * start_gain)[..., None] * key_rows], -1
    )
    solved = jax.scipy.linalg.solve_triangular(system, right_side, lower=True, unit_diagonal=True)
    written = solved[..., :head_depth]
    erased = solved[..., head_depth:]
    scores = (
        jnp.einsum("hcrd,hcjd->hcrj", read_rows, key_rows, precision=PRECISE_SETTING)
        * decay_ratio[:, :, 1::2, :]
    )
    inner_out = jnp.einsum("hcrj,hcje->hcre", scores, written, precision=PRECISE_SETTING)
    carried = start_gain[:, :, 1::2, None] * read_rows - jnp.einsum(
        "hcrj,hcje->hcre", scores, erased, precision=PRECISE_SETTING
    )
    weighted = end_gain[..., None] * key_rows
    identity_map = jnp.broadcast_to(
        jnp.eye(head_depth, dtype=jnp.float32), (heads_here, head_depth, head_depth)
    )
    transition = start_gain[..., -1, None, None] * identity_map[:, None] - jnp.einsum(
        "hcid,hcie->hcde", weighted, erased, precision=PRECISE_SETTING
    )
    fresh_state = jnp.einsum("hcid,hcie->hcde", weighted, written, precision=PRECISE_SETTING)
    zero_state = jnp.zeros((heads_here, head_depth, head_depth), jnp.float32)
    ends_pair, starts_pair = lax.scan(
        advance,
        (zero_state, identity_map),
        (transition.transpose(1, 0, 2, 3), fresh_state.transpose(1, 0, 2, 3)),
    )
    local_end, local_map = ends_pair
    block_starts, block_maps = starts_pair
    return (inner_out, carried, block_starts, block_maps, local_end, local_map)


def finish_readout(inner_out, carried, block_starts, block_maps, incoming):
    heads_here = inner_out.shape[0]
    head_depth = inner_out.shape[-1]
    begin_state = block_starts + jnp.einsum(
        "chde,hef->chdf", block_maps, incoming, precision=PRECISE_SETTING
    )
    readout = inner_out + jnp.einsum(
        "hcrd,chde->hcre", carried, begin_state, precision=PRECISE_SETTING
    )
    return readout.reshape(heads_here, -1, head_depth).transpose(1, 0, 2)


def norm_rows(readout, gate_part, norm_gain):
    group_len, heads_here, head_depth = readout.shape
    gate_vals = gate_part.reshape(group_len, heads_here, head_depth).astype(jnp.float32)
    inv_rms = lax.rsqrt(jnp.mean(readout * readout, -1, keepdims=True) + 1e-05)
    normed = (readout * inv_rms * norm_gain * jax.nn.silu(gate_vals)).astype(jnp.bfloat16)
    return normed.reshape(group_len, heads_here * head_depth)


def chain_states(local_map, local_end):
    heads_here, head_depth = (local_map.shape[0], local_map.shape[1])
    zero_state = jnp.zeros((heads_here, head_depth, head_depth), jnp.float32)

    def relay_once(turn_index, incoming):
        outgoing = (
            jnp.einsum("hde,hef->hdf", local_map, incoming, precision=PRECISE_SETTING) + local_end
        )
        return passed_along(outgoing.astype(jnp.bfloat16), "seq", 1).astype(outgoing.dtype)

    incoming = lax.fori_loop(0, lax.axis_size("seq") - 1, relay_once, zero_state)
    return incoming


def on_device(
    queries, keys, values, out_gate, write_rate, log_decay, doc_starts, norm_gain, out_weight
):
    tok_dev, feature_width = queries.shape
    heads_all = log_decay.shape[1]
    groups = lax.axis_size("head")
    local_heads = heads_all // groups
    head_depth = feature_width // heads_all
    arrived = (
        lax.all_to_all(queries[:, None, :], "head", split_axis=2, concat_axis=0, tiled=True),
        lax.all_to_all(keys, "head", split_axis=2, concat_axis=0, tiled=True),
        lax.all_to_all(values, "head", split_axis=2, concat_axis=0, tiled=True),
        lax.all_to_all(out_gate[:, None, :], "head", split_axis=2, concat_axis=0, tiled=True),
        lax.all_to_all(write_rate, "head", split_axis=2, concat_axis=0, tiled=True),
        lax.all_to_all(log_decay[:, None, :], "head", split_axis=2, concat_axis=0, tiled=True),
    )
    query_part, key_part, value_part, gate_part, rate_part, decay_part = arrived
    group_len = query_part.shape[0]
    first_pos = lax.axis_index("seq") * group_len
    inner_out, carried, block_starts, block_maps, local_end, local_map = stretch_pieces(
        query_part,
        key_part,
        value_part,
        rate_part,
        decay_part,
        first_pos,
        doc_starts,
        local_heads,
        head_depth,
    )
    incoming = chain_states(local_map, local_end)
    readout = finish_readout(inner_out, carried, block_starts, block_maps, incoming)
    normed = norm_rows(readout, gate_part, norm_gain)
    acc_total = jnp.dot(
        lax.all_gather(normed, "head", axis=1, tiled=True),
        out_weight,
        preferred_element_type=jnp.float32,
    )
    return acc_total.astype(jnp.bfloat16)


def solution(mesh):
    placed = (
        P(("rep", "seq", "head"), None),
        P(("rep", "seq", "head"), None, None),
        P(("rep", "seq", "head"), None, None),
        P(("rep", "seq", "head"), None),
        P(("rep", "seq", "head"), None, None),
        P(("rep", "seq", "head"), None),
        P("rep"),
        P(),
        P(None, "head"),
    )
    return jax.shard_map(
        on_device, mesh=mesh, in_specs=placed, out_specs=P(("rep", "seq"), "head"), check_vma=False
    )
```

profile of v0, /device:TPU:0, one launch (start us, length us, event | category | flops | bytes accessed | tf_op | source)
XLA Modules:
  0.0 342.5 jit_solution(240848373415669369)
XLA Ops:
  8.0 4.2 %all-to-all-start.2 = ((bf16[4,2,128]{2,1,0:T(2,128)(2,1)}), bf16[4,2,128]{2,1,0:T(2,128)(2,1)S(1)}, u32[]{:S(2)}, u32[]{:S(2)}) async-start(bf16[4,2,128]{2,1,0:T(2,128)(2,1)} %bitcast.133), calls=%async_computation.2 | async-start | bytes 4096 | tf_op jit(solution)/shard_map/all_to_all | solution.py:162
  21.4 2.2 reduce.6
  28.5 2.2 reduce.7
  31.4 3.3 all-to-all-start.3
  35.8 2.7 all-to-all-done.3
  38.5 3.4 all-to-all-start.1
  43.9 4.0 %all-to-all-done.1 = bf16[4,2,16384]{2,1,0:T(2,128)(2,1)S(1)} async-done(((bf16[4,2,16384]{2,1,0:T(2,128)(2,1)}), bf16[4,2,16384]{2,1,0:T(2,128)(2,1)S(1)}, u32[]{:S(2)}, u32[]{:S(2)}) %all-to-all-start.1) | async-done | bytes 262176 | tf_op jit(solution)/shard_map/all_to_all | solution.py:157
  47.9 3.4 all-to-all-start.5
  51.9 5.5 %all-to-all-done.5 = bf16[4,2,16384]{2,1,0:T(2,128)(2,1)S(1)} async-done(((bf16[4,2,16384]{2,1,0:T(2,128)(2,1)}), bf16[4,2,16384]{2,1,0:T(2,128)(2,1)S(1)}, u32[]{:S(2)}, u32[]{:S(2)}) %all-to-all-start.5) | async-done | bytes 262176 | tf_op jit(solution)/shard_map/all_to_all | solution.py:160
  57.3 3.5 %all-to-all-start = ((bf16[128,2,1024]{0,1,2:T(2,128)(2,1)}), bf16[128,2,1024]{0,1,2:T(2,128)(2,1)S(1)}, u32[]{:S(2)}, u32[]{:S(2)}) async-start(bf16[128,2,1024]{0,1,2:T(2,128)(2,1)} %copy.164), calls=%async_computation | async-start | bytes 1048576 | tf_op jit(solution)/shard_map/all_to_all | solution.py:158
  66.3 3.3 all-to-all-done
  69.6 4.1 %all-to-all-start.4 = ((bf16[128,2,1024]{0,1,2:T(2,128)(2,1)}), bf16[128,2,1024]{0,1,2:T(2,128)(2,1)}, u32[]{:S(2)}, u32[]{:S(2)}) async-start(bf16[128,2,1024]{0,1,2:T(2,128)(2,1)} %copy.177), calls=%async_computation.4 | async-start | bytes 1048576 | tf_op jit(solution)/shard_map/all_to_all | solution.py:159
  78.5 4.2 %all-to-all-done.4 = bf16[128,2,1024]{0,1,2:T(2,128)(2,1)} async-done(((bf16[128,2,1024]{0,1,2:T(2,128)(2,1)}), bf16[128,2,1024]{0,1,2:T(2,128)(2,1)}, u32[]{:S(2)}, u32[]{:S(2)}) %all-to-all-start.4) | async-done | bytes 524320 | tf_op jit(solution)/shard_map/all_to_all | solution.py:159
  85.6 3.0 copy.179
  88.7 3.4 %fusion.26 = f32[2,8,1,128,128]{4,3,2,1,0:T(8,128)} fusion(f32[2,8,128,128]{3,2,1,0:T(8,128)S(1)} %bitcast.148, f32[128,128]{1,0:T(8,128)S(1)} %copy-done.16, f32[128,128]{1,0:T(8,128)S(1)} %copy-done.7, f32[2,8,128]{2,1,0:T(8,128)S(1)} %copy-done.15, pred[128,128]{1,0:T(8,128)(4,1)S(1)} %copy-done.19, pred[128,128]{1,0:T(8,128)(4,1)S(1)} %copy-done.20, ...), kind=kOutput, calls=%fused_computation.35 | convolution fusion | flops 405012480 | bytes 2408448 | tf_op jit(solution)/shard_map/hcid,hcjd->hcij/dot_general | solution.py:78
  92.2 158.6 %custom-call.4 = f32[2,8,1,128,128]{3,4,2,1,0:T(8,128)} custom-call(f32[2,8,1,128,128]{4,3,2,1,0:T(8,128)} %fusion.26), custom_call_target="InvertDiagBlocksLowerTriangular" | custom-call | tf_op jit(solution)/shard_map/jit(_solve_triangular)/vmap(vmap())/triangular_solve | solution.py:84
  250.8 2.3 fusion.27
  254.4 2.0 fusion.16
  256.4 1.9 fusion.33
  258.3 1.9 convolution_subtract_fusion
  260.2 3.2 convolution_bitcast_fusion.1
  263.4 2.2 fusion.21
  265.7 23.6 %while.28 = (s32[]{:T(128)}, f32[2,128,128]{2,1,0:T(8,128)S(1)}, f32[2,128,128]{2,1,0:T(8,128)S(1)}, f32[8,2,128,128]{2,3,1,0:T(8,128)}, f32[8,2,128,128]{3,2,1,...) while((s32[]{:T(128)}, f32[2,128,128]{2,1,0:T(8,128)S(1)}, ...), condition=%wide.region_5.6_spmd.clone, body=%wide.region_4.5_spmd.clone.sunk | while | flops 100761600 | bytes 2492027 | solution.py:104
  289.3 19.3 %while.29 = (s32[]{:T(128)}, f32[2,128,128]{2,1,0:T(8,128)S(1)}, f32[2,128,128]{2,1,0:T(8,128)S(1)}, f32[2,128,128]{2,1,0:T(8,128)S(1)}, s32[]{:T(128)}, /*index=5*/s32[]{:T(128)}) while((s32[]{:T(128)}, f32[2,128,128]{2,1,0:T(8,128)S(1)}, f32[2,128,128]{2,1,0:T(8,128)S(1)}, f32[2,128,128]{2,1,0:T(8,128)S(1)}, s32[]{:T(128)}, ...), condition=%wide.region_7.8_spmd.clone, body=%wide.region_6.7_spmd.clone.sunk | while | flops 50462720 | bytes 917623 | solution.py:144
  289.6 3.9 %collective-permute-start = (bf16[2,128,128]{2,1,0:T(8,128)(2,1)S(1)}, bf16[2,128,128]{2,1,0:T(8,128)(2,1)S(1)}, u32[]{:S(2)}, u32[]{:S(2)}) collective-permute-start(bf16[2,128,128]{2,1,0:T(8,128)(2,1)S(1)} %fusion.76), channel_id=1, source_target_pairs={{0,4},{4,8},{8,12},{1,5},{5,9},{9,13},{2,6},{6,10},{10,14},{3,7},{... | collective-permute-start | bytes 196616 | tf_op jit(solution)/shard_map/while/body/eval_jaxpr/ppermute | solution.py:13
  293.6 1.9 collective-permute-done
  295.8 4.3 %collective-permute-start = (bf16[2,128,128]{2,1,0:T(8,128)(2,1)S(1)}, bf16[2,128,128]{2,1,0:T(8,128)(2,1)S(1)}, u32[]{:S(2)}, u32[]{:S(2)}) collective-permute-start(bf16[2,128,128]{2,1,0:T(8,128)(2,1)S(1)} %fusion.76), channel_id=1, source_target_pairs={{0,4},{4,8},{8,12},{1,5},{5,9},{9,13},{2,6},{6,10},{10,14},{3,7},{... | collective-permute-start | bytes 196616 | tf_op jit(solution)/shard_map/while/body/eval_jaxpr/ppermute | solution.py:13
  302.2 4.3 %collective-permute-start = (bf16[2,128,128]{2,1,0:T(8,128)(2,1)S(1)}, bf16[2,128,128]{2,1,0:T(8,128)(2,1)S(1)}, u32[]{:S(2)}, u32[]{:S(2)}) collective-permute-start(bf16[2,128,128]{2,1,0:T(8,128)(2,1)S(1)} %fusion.76), channel_id=1, source_target_pairs={{0,4},{4,8},{8,12},{1,5},{5,9},{9,13},{2,6},{6,10},{10,14},{3,7},{... | collective-permute-start | bytes 196616 | tf_op jit(solution)/shard_map/while/body/eval_jaxpr/ppermute | solution.py:13
  308.7 2.7 fusion.20
  311.4 2.1 convolution_add_fusion.2
  314.9 18.0 %all-gather.2.cloned.1.call-done = bf16[512,1024]{0,1:T(8,128)(2,1)} async-done(((bf16[512,256]{0,1:T(8,128)(2,1)}), bf16[512,1024]{0,1:T(8,128)(2,1)}) %all-gather.2.cloned.1.call-update) | async-done | bytes 1048592 | tf_op jit(solution)/shard_map/all_gather | solution.py:182
  332.9 2.8 convolution_convert_fusion
  (196 shorter events, 62.4 us)
Async XLA Ops:
  6.5 326.4 %copy-start = (bf16[1024,512]{1,0:T(8,128)(2,1)S(1)}, bf16[1024,512]{1,0:T(8,128)(2,1)}, u32[]{:S(2)}) copy-start(bf16[1024,512]{1,0:T(8,128)(2,1)} %param.21) | copy-start | bytes 3145732
  6.5 17.8 %copy-start.11 = (bf16[128,2,1024]{2,1,0:T(2,128)(2,1)S(1)}, bf16[128,2,1024]{2,1,0:T(2,128)(2,1)}, u32[]{:S(2)}) copy-start(bf16[128,2,1024]{2,1,0:T(2,128)(2,1)} %param.14) | copy-start | bytes 1572868
  6.5 19.7 %copy-start.12 = (bf16[128,2,1024]{2,1,0:T(2,128)(2,1)S(1)}, bf16[128,2,1024]{2,1,0:T(2,128)(2,1)}, u32[]{:S(2)}) copy-start(bf16[128,2,1024]{2,1,0:T(2,128)(2,1)} %param.15) | copy-start | bytes 1572868
  8.0 23.5 %all-to-all-start.2 = ((bf16[4,2,128]{2,1,0:T(2,128)(2,1)}), bf16[4,2,128]{2,1,0:T(2,128)(2,1)S(1)}, u32[]{:S(2)}, u32[]{:S(2)}) async-start(bf16[4,2,128]{2,1,0:T(2,128)(2,1)} %bitcast.133), calls=%async_computation.2 | async-start | bytes 4096 | tf_op jit(solution)/shard_map/all_to_all | solution.py:162
  16.9 25.1 %copy-start.9 = (pred[8,128,128]{2,1,0:T(8,128)(4,1)}, pred[8,128,128]{2,1,0:T(8,128)(4,1)S(1)}, u32[]{:S(2)}) copy-start(pred[8,128,128]{2,1,0:T(8,128)(4,1)S(1)} %compare_and_fusion) | copy-start | bytes 393220
  19.5 8.6 %copy-start.13 = (bf16[128,1024]{1,0:T(8,128)(2,1)S(1)}, bf16[128,1024]{1,0:T(8,128)(2,1)}, u32[]{:S(2)}) copy-start(bf16[128,1024]{1,0:T(8,128)(2,1)} %param.16) | copy-start | bytes 786436
  31.4 7.1 %all-to-all-start.3 = ((bf16[128,2,8]{0,1,2:T(2,128)(2,1)}), bf16[128,2,8]{0,1,2:T(2,128)(2,1)S(1)}, u32[]{:S(2)}, u32[]{:S(2)}) async-start(bf16[128,2,8]{0,1,2:T(2,128)(2,1)} %copy.175), calls=%async_computation.3 | async-start | bytes 8192 | tf_op jit(solution)/shard_map/all_to_all | solution.py:161
  38.5 9.4 %all-to-all-start.1 = ((bf16[4,2,16384]{2,1,0:T(2,128)(2,1)}), bf16[4,2,16384]{2,1,0:T(2,128)(2,1)S(1)}, u32[]{:S(2)}, u32[]{:S(2)}) async-start(bf16[4,2,16384]{2,1,0:T(2,128)(2,1)} %reshape.194), calls=%async_computation.1 | async-start | bytes 524288 | tf_op jit(solution)/shard_map/all_to_all | solution.py:157
  42.3 18.5 %copy-start.22 = (pred[8,128]{1,0:T(8,128)(4,1)S(1)}, pred[8,128]{1,0:T(8,128)(4,1)}, u32[]{:S(2)}) copy-start(pred[8,128]{1,0:T(8,128)(4,1)} %copy.182) | copy-start | bytes 3076
  42.3 18.5 %copy-start.23 = (pred[8,128]{1,0:T(8,128)(4,1)S(1)}, pred[8,128]{1,0:T(8,128)(4,1)}, u32[]{:S(2)}) copy-start(pred[8,128]{1,0:T(8,128)(4,1)} %copy.180) | copy-start | bytes 3076
  47.9 9.4 %all-to-all-start.5 = ((bf16[4,2,16384]{2,1,0:T(2,128)(2,1)}), bf16[4,2,16384]{2,1,0:T(2,128)(2,1)S(1)}, u32[]{:S(2)}, u32[]{:S(2)}) async-start(bf16[4,2,16384]{2,1,0:T(2,128)(2,1)} %reshape.196), calls=%async_computation.5 | async-start | bytes 524288 | tf_op jit(solution)/shard_map/all_to_all | solution.py:160
  51.8 11.4 %copy-start.14 = (f32[2,8,128]{2,1,0:T(8,128)}, f32[2,8,128]{2,1,0:T(8,128)S(1)}, u32[]{:S(2)}) copy-start(f32[2,8,128]{2,1,0:T(8,128)S(1)} %reshape.172) | copy-start | bytes 24580
  57.3 12.3 %all-to-all-start = ((bf16[128,2,1024]{0,1,2:T(2,128)(2,1)}), bf16[128,2,1024]{0,1,2:T(2,128)(2,1)S(1)}, u32[]{:S(2)}, u32[]{:S(2)}) async-start(bf16[128,2,1024]{0,1,2:T(2,128)(2,1)} %copy.164), calls=%async_computation | async-start | bytes 1048576 | tf_op jit(solution)/shard_map/all_to_all | solution.py:158
  69.6 13.1 %all-to-all-start.4 = ((bf16[128,2,1024]{0,1,2:T(2,128)(2,1)}), bf16[128,2,1024]{0,1,2:T(2,128)(2,1)}, u32[]{:S(2)}, u32[]{:S(2)}) async-start(bf16[128,2,1024]{0,1,2:T(2,128)(2,1)} %copy.177), calls=%async_computation.4 | async-start | bytes 1048576 | tf_op jit(solution)/shard_map/all_to_all | solution.py:159
  73.8 259.1 %all-gather.2.cloned.1.call-start = ((), (), s32[]{:S(2)}) async-start(), calls=%async_computation.6 | async-start | bytes 1310720 | tf_op jit(solution)/shard_map/all_gather | solution.py:182
  84.1 4.6 %copy-start.7 = (f32[128,128]{1,0:T(8,128)S(1)}, f32[128,128]{1,0:T(8,128)}, u32[]{:S(2)}) copy-start(f32[128,128]{1,0:T(8,128)} %get-tuple-element.189) | copy-start | bytes 196612
  84.1 4.6 %copy-start.15 = (f32[2,8,128]{2,1,0:T(8,128)S(1)}, f32[2,8,128]{2,1,0:T(8,128)}, u32[]{:S(2)}) copy-start(f32[2,8,128]{2,1,0:T(8,128)} %copy-done.14) | copy-start | bytes 24580
  84.1 4.6 %copy-start.19 = (pred[128,128]{1,0:T(8,128)(4,1)S(1)}, pred[128,128]{1,0:T(8,128)(4,1)}, u32[]{:S(2)}) copy-start(pred[128,128]{1,0:T(8,128)(4,1)} %get-tuple-element.187) | copy-start | bytes 49156
  84.1 4.6 %copy-start.20 = (pred[128,128]{1,0:T(8,128)(4,1)S(1)}, pred[128,128]{1,0:T(8,128)(4,1)}, u32[]{:S(2)}) copy-start(pred[128,128]{1,0:T(8,128)(4,1)} %get-tuple-element.188) | copy-start | bytes 49156
  85.6 3.1 copy-start.10
  85.6 3.1 copy-start.16
  88.7 162.1 %copy-start.2 = (bf16[2,512,128]{2,1,0:T(8,128)(2,1)S(1)}, bf16[2,512,128]{2,1,0:T(8,128)(2,1)}, u32[]{:S(2)}) copy-start(bf16[2,512,128]{2,1,0:T(8,128)(2,1)} %copy.169) | copy-start | bytes 786436
  92.2 161.0 %copy-start.18 = (f32[2,8,128]{2,1,0:T(8,128)S(1)}, f32[2,8,128]{2,1,0:T(8,128)}, u32[]{:S(2)}) copy-start(f32[2,8,128]{2,1,0:T(8,128)} %get-tuple-element.182) | copy-start | bytes 24580
  260.2 3.2 copy-start.8
  260.2 3.2 copy-start.21
  289.6 5.8 %collective-permute-start = (bf16[2,128,128]{2,1,0:T(8,128)(2,1)S(1)}, bf16[2,128,128]{2,1,0:T(8,128)(2,1)S(1)}, u32[]{:S(2)}, u32[]{:S(2)}) collective-permute-start(bf16[2,128,128]{2,1,0:T(8,128)(2,1)S(1)} %fusion.76), channel_id=1, source_target_pairs={{0,4},{4,8},{8,12},{1,5},{5,9},{9,13},{2,6},{6,10},{10,14},{3,7},{... | collective-permute-start | bytes 196616 | tf_op jit(solution)/shard_map/while/body/eval_jaxpr/ppermute | solution.py:13
  295.8 6.2 %collective-permute-start = (bf16[2,128,128]{2,1,0:T(8,128)(2,1)S(1)}, bf16[2,128,128]{2,1,0:T(8,128)(2,1)S(1)}, u32[]{:S(2)}, u32[]{:S(2)}) collective-permute-start(bf16[2,128,128]{2,1,0:T(8,128)(2,1)S(1)} %fusion.76), channel_id=1, source_target_pairs={{0,4},{4,8},{8,12},{1,5},{5,9},{9,13},{2,6},{6,10},{10,14},{3,7},{... | collective-permute-start | bytes 196616 | tf_op jit(solution)/shard_map/while/body/eval_jaxpr/ppermute | solution.py:13
  302.2 6.2 %collective-permute-start = (bf16[2,128,128]{2,1,0:T(8,128)(2,1)S(1)}, bf16[2,128,128]{2,1,0:T(8,128)(2,1)S(1)}, u32[]{:S(2)}, u32[]{:S(2)}) collective-permute-start(bf16[2,128,128]{2,1,0:T(8,128)(2,1)S(1)} %fusion.76), channel_id=1, source_target_pairs={{0,4},{4,8},{8,12},{1,5},{5,9},{9,13},{2,6},{6,10},{10,14},{3,7},{... | collective-permute-start | bytes 196616 | tf_op jit(solution)/shard_map/while/body/eval_jaxpr/ppermute | solution.py:13
  308.7 2.7 copy-start.4
  308.7 2.7 copy-start.5
  311.4 2.4 copy-start.3
  311.4 2.4 copy-start.24
  (3 other events, 5.5 us)
Sparse Core Ops, SparseCore 0:
  315.0 17.8 all-gather.1
where the time goes:
time: 344 us; the launch traced here: 343 us
  other arithmetic  173 us (50%)
  waiting for transfers between devices  43.3 us (13%)
  local copies, waits for them, and re-layouts  39.4 us (11%)
  matrix products  36.9 us (11%)
  starting transfers between devices  34.6 us (10%)
  between operations  14.7 us (4%)
    another operation x2, other arithmetic, stretch_pieces(): jax.scipy.linalg.solve_triangular(system, right_side, lower=True, unit_di...  159 us
    all_gather x1, waiting for transfers between devices, on_device(): lax.all_gather(normed, 'head', axis=1, tiled=True)  18 us
    ppermute x3, starting transfers between devices, passed_along(): lax.ppermute(value, axis, [(source, source + steps) for source in range(i...  12.5 us
    dynamic_update_slice x24, local copies, waits for them, and re-layouts, stretch_pieces(): lax.scan(advance, (zero_state, identity_map), (transition.transpose(1, 0,...  11.3 us
    dot_general x8, matrix products, advance(): jnp.einsum('hde,hef->hdf', step_map, current_state, precision=PRECISE_SET...  9.44 us
    unnamed x62, local copies, waits for them, and re-layouts  8.95 us
  transfers between devices with their start and end apart: 10, of which 9 were waited for; matrix products, arithmetic and copies ran while one was open for 9% of the time, Pallas kernels for 0%

commit v1 on v0

--- a/solution.py
+++ b/solution.py
@@ -5,6 +5,28 @@
 from jax.sharding import PartitionSpec as P
 
 PRECISE_SETTING = lax.Precision.HIGHEST
+
+
+def cut_along(x, dim, size):
+    before, after = (x.shape[:dim], x.shape[dim + 1 :])
+    return jnp.moveaxis(x.reshape(*before, size, -1, *after), dim, 0)
+
+
+def joined_along(blocks, dim):
+    lengths = list(blocks.shape[1:])
+    lengths[dim] *= blocks.shape[0]
+    return jnp.moveaxis(blocks, 0, dim).reshape(lengths)
+
+
+def rotated_exchange(array, axis, split_dim, concat_dim):
+    size, index = (lax.axis_size(axis), lax.axis_index(axis))
+    blocks = cut_along(array, split_dim, size)
+    outs = [blocks[index]]
+    for hop in range(1, size):
+        sent = blocks[(index + hop) % size]
+        outs.append(lax.ppermute(sent, axis, [(i, (i + hop) % size) for i in range(size)]))
+    blocks = jnp.stack(outs)[(index - jnp.arange(size)) % size]
+    return joined_along(blocks, concat_dim)
 
 
 def passed_along(value, axis, steps):
@@ -154,7 +176,7 @@
     local_heads = heads_all // groups
     head_depth = feature_width // heads_all
     arrived = (
-        lax.all_to_all(queries[:, None, :], "head", split_axis=2, concat_axis=0, tiled=True),
+        rotated_exchange(queries[:, None, :], "head", 2, 0),
         lax.all_to_all(keys, "head", split_axis=2, concat_axis=0, tiled=True),
         lax.all_to_all(values, "head", split_axis=2, concat_axis=0, tiled=True),
         lax.all_to_all(out_gate[:, None, :], "head", split_axis=2, concat_axis=0, tiled=True),

time: 344 us -> 332 us (0.965)
  waiting for transfers between devices: 43.3 us -> 37.2 us
    all_to_all x1 -> x0, waiting for transfers between devices: 4.01 us -> none  [on_device(): lax.all_to_all(queries[:, None, :], 'head', split_axis=2, concat_axis=0,...]
    ppermute x0 -> x3, starting transfers between devices: none -> 3.66 us  [rotated_exchange(): lax.ppermute(sent, axis, [(i, (i + hop) % size) for i in range(size)])]
    unnamed x62 -> x56, local copies, waits for them, and re-layouts: 8.95 us -> 8.41 us
  transfers between devices with their start and end apart: 10 -> 12, of which waited for: 9 -> 8; matrix products, arithmetic and copies ran while one was open for 9% -> 8% of each run, Pallas kernels for 0% -> 0%
where the time goes in v1:
time: 332 us
  other arithmetic  171 us (52%)
  waiting for transfers between devices  37.2 us (11%)
  matrix products  36.9 us (11%)
  local copies, waits for them, and re-layouts  36.4 us (11%)
  starting transfers between devices  34.8 us (10%)
  between operations  14.7 us (4%)
    another operation x2, other arithmetic, stretch_pieces(): jax.scipy.linalg.solve_triangular(system, right_side, lower=True, unit_di...  159 us
    all_gather x1, waiting for transfers between devices, on_device(): lax.all_gather(normed, 'head', axis=1, tiled=True)  18 us
    ppermute x3, starting transfers between devices, passed_along(): lax.ppermute(value, axis, [(source, source + steps) for source in range(i...  12.5 us
    dynamic_update_slice x24, local copies, waits for them, and re-layouts, stretch_pieces(): lax.scan(advance, (zero_state, identity_map), (transition.transpose(1, 0,...  11.4 us
    dot_general x8, matrix products, advance(): jnp.einsum('hde,hef->hdf', step_map, current_state, precision=PRECISE_SET...  9.44 us
    unnamed x56, local copies, waits for them, and re-layouts  8.41 us
  transfers between devices with their start and end apart: 12, of which 8 were waited for; matrix products, arithmetic and copies ran while one was open for 8% of the time, Pallas kernels for 0%

profile of v1, /device:TPU:0, one launch (start us, length us, event | category | flops | bytes accessed | tf_op | source)
XLA Modules:
  0.0 331.6 jit_solution(3225652230286875750)
XLA Ops:
  8.0 4.2 %all-to-all-start.1 = ((bf16[4,2,128]{2,1,0:T(2,128)(2,1)}), bf16[4,2,128]{2,1,0:T(2,128)(2,1)S(1)}, u32[]{:S(2)}, u32[]{:S(2)}) async-start(bf16[4,2,128]{2,1,0:T(2,128)(2,1)} %bitcast.131), calls=%async_computation.1 | async-start | bytes 4096 | tf_op jit(solution)/shard_map/all_to_all | solution.py:184
  23.1 1.9 copy.211
  25.0 1.9 copy.221
  27.8 2.2 reduce.6
  30.8 3.2 all-to-all-start.2
  37.8 3.4 %all-to-all-start.4 = ((bf16[4,2,16384]{2,1,0:T(2,128)(2,1)}), bf16[4,2,16384]{2,1,0:T(2,128)(2,1)S(1)}, u32[]{:S(2)}, u32[]{:S(2)}) async-start(bf16[4,2,16384]{2,1,0:T(2,128)(2,1)} %reshape.256), calls=%async_computation.4 | async-start | bytes 524288 | tf_op jit(solution)/shard_map/all_to_all | solution.py:182
  42.3 4.9 %all-to-all-done.4 = bf16[4,2,16384]{2,1,0:T(2,128)(2,1)S(1)} async-done(((bf16[4,2,16384]{2,1,0:T(2,128)(2,1)}), bf16[4,2,16384]{2,1,0:T(2,128)(2,1)S(1)}, u32[]{:S(2)}, u32[]{:S(2)}) %all-to-all-start.4) | async-done | bytes 262176 | tf_op jit(solution)/shard_map/all_to_all | solution.py:182
  47.2 3.5 %all-to-all-start = ((bf16[128,2,1024]{0,1,2:T(2,128)(2,1)}), bf16[128,2,1024]{0,1,2:T(2,128)(2,1)S(1)}, u32[]{:S(2)}, u32[]{:S(2)}) async-start(bf16[128,2,1024]{0,1,2:T(2,128)(2,1)} %copy.211), calls=%async_computation | async-start | bytes 1048576 | tf_op jit(solution)/shard_map/all_to_all | solution.py:180
  55.7 3.8 %all-to-all-done = bf16[128,2,1024]{0,1,2:T(2,128)(2,1)S(1)} async-done(((bf16[128,2,1024]{0,1,2:T(2,128)(2,1)}), bf16[128,2,1024]{0,1,2:T(2,128)(2,1)S(1)}, u32[]{:S(2)}, u32[]{:S(2)}) %all-to-all-start) | async-done | bytes 524320 | tf_op jit(solution)/shard_map/all_to_all | solution.py:180
  59.5 4.2 %all-to-all-start.3 = ((bf16[128,2,1024]{0,1,2:T(2,128)(2,1)}), bf16[128,2,1024]{0,1,2:T(2,128)(2,1)}, u32[]{:S(2)}, u32[]{:S(2)}) async-start(bf16[128,2,1024]{0,1,2:T(2,128)(2,1)} %copy.221), calls=%async_computation.3 | async-start | bytes 1048576 | tf_op jit(solution)/shard_map/all_to_all | solution.py:181
  68.4 4.2 %all-to-all-done.3 = bf16[128,2,1024]{0,1,2:T(2,128)(2,1)} async-done(((bf16[128,2,1024]{0,1,2:T(2,128)(2,1)}), bf16[128,2,1024]{0,1,2:T(2,128)(2,1)}, u32[]{:S(2)}, u32[]{:S(2)}) %all-to-all-start.3) | async-done | bytes 524320 | tf_op jit(solution)/shard_map/all_to_all | solution.py:181
  75.5 2.1 copy.223
  77.7 3.4 %fusion.26 = f32[2,8,1,128,128]{4,3,2,1,0:T(8,128)} fusion(f32[2,8,128,128]{3,2,1,0:T(8,128)S(1)} %bitcast.146, f32[128,128]{1,0:T(8,128)S(1)} %copy-done.15, f32[128,128]{1,0:T(8,128)S(1)} %copy-done.6, f32[2,8,128]{2,1,0:T(8,128)S(1)} %copy-done.14, pred[128,128]{1,0:T(8,128)(4,1)S(1)} %copy-done.18, pred[128,128]{1,0:T(8,128)(4,1)S(1)} %copy-done.19, ...), kind=kOutput, calls=%fused_computation.36 | convolution fusion | flops 405012480 | bytes 2408448 | tf_op jit(solution)/shard_map/hcid,hcjd->hcij/dot_general | solution.py:100
  81.1 158.7 %custom-call.4 = f32[2,8,1,128,128]{3,4,2,1,0:T(8,128)} custom-call(f32[2,8,1,128,128]{4,3,2,1,0:T(8,128)} %fusion.26), custom_call_target="InvertDiagBlocksLowerTriangular" | custom-call | tf_op jit(solution)/shard_map/jit(_solve_triangular)/vmap(vmap())/triangular_solve | solution.py:106
  239.8 2.3 convolution_multiply_fusion.1
  243.3 2.0 fusion.16
  245.3 1.9 fusion.32
  247.2 1.9 convolution_subtract_fusion
  249.1 3.2 convolution_bitcast_fusion.1
  252.3 2.2 fusion.21
  254.6 23.8 %while.28 = (s32[]{:T(128)}, f32[2,128,128]{2,1,0:T(8,128)S(1)}, f32[2,128,128]{2,1,0:T(8,128)S(1)}, f32[8,2,128,128]{2,3,1,0:T(8,128)}, f32[8,2,128,128]{3,2,1,...) while((s32[]{:T(128)}, f32[2,128,128]{2,1,0:T(8,128)S(1)}, ...), condition=%wide.region_5.6_spmd.clone, body=%wide.region_4.5_spmd.clone.sunk | while | flops 100761600 | bytes 2492027 | solution.py:126
  278.4 19.4 %while.29 = (s32[]{:T(128)}, f32[2,128,128]{2,1,0:T(8,128)S(1)}, f32[2,128,128]{2,1,0:T(8,128)S(1)}, f32[2,128,128]{2,1,0:T(8,128)S(1)}, s32[]{:T(128)}, /*index=5*/s32[]{:T(128)}) while((s32[]{:T(128)}, f32[2,128,128]{2,1,0:T(8,128)S(1)}, f32[2,128,128]{2,1,0:T(8,128)S(1)}, f32[2,128,128]{2,1,0:T(8,128)S(1)}, s32[]{:T(128)}, ...), condition=%wide.region_7.8_spmd.clone, body=%wide.region_6.7_spmd.clone.sunk | while | flops 50462720 | bytes 917623 | solution.py:166
  278.7 4.0 %collective-permute-start = (bf16[2,128,128]{2,1,0:T(8,128)(2,1)S(1)}, bf16[2,128,128]{2,1,0:T(8,128)(2,1)S(1)}, u32[]{:S(2)}, u32[]{:S(2)}) collective-permute-start(bf16[2,128,128]{2,1,0:T(8,128)(2,1)S(1)} %fusion.77), channel_id=1, source_target_pairs={{0,4},{4,8},{8,12},{1,5},{5,9},{9,13},{2,6},{6,10},{10,14},{3,7},{... | collective-permute-start | bytes 196616 | tf_op jit(solution)/shard_map/while/body/eval_jaxpr/ppermute | solution.py:35
  282.6 1.9 collective-permute-done
  284.8 4.3 %collective-permute-start = (bf16[2,128,128]{2,1,0:T(8,128)(2,1)S(1)}, bf16[2,128,128]{2,1,0:T(8,128)(2,1)S(1)}, u32[]{:S(2)}, u32[]{:S(2)}) collective-permute-start(bf16[2,128,128]{2,1,0:T(8,128)(2,1)S(1)} %fusion.77), channel_id=1, source_target_pairs={{0,4},{4,8},{8,12},{1,5},{5,9},{9,13},{2,6},{6,10},{10,14},{3,7},{... | collective-permute-start | bytes 196616 | tf_op jit(solution)/shard_map/while/body/eval_jaxpr/ppermute | solution.py:35
  289.1 1.9 collective-permute-done
  291.3 4.3 %collective-permute-start = (bf16[2,128,128]{2,1,0:T(8,128)(2,1)S(1)}, bf16[2,128,128]{2,1,0:T(8,128)(2,1)S(1)}, u32[]{:S(2)}, u32[]{:S(2)}) collective-permute-start(bf16[2,128,128]{2,1,0:T(8,128)(2,1)S(1)} %fusion.77), channel_id=1, source_target_pairs={{0,4},{4,8},{8,12},{1,5},{5,9},{9,13},{2,6},{6,10},{10,14},{3,7},{... | collective-permute-start | bytes 196616 | tf_op jit(solution)/shard_map/while/body/eval_jaxpr/ppermute | solution.py:35
  295.6 1.9 collective-permute-done
  297.8 2.7 fusion.20
  300.5 2.1 convolution_add_fusion.2
  304.0 18.0 %all-gather.2.cloned.1.call-done = bf16[512,1024]{0,1:T(8,128)(2,1)} async-done(((bf16[512,256]{0,1:T(8,128)(2,1)}), bf16[512,1024]{0,1:T(8,128)(2,1)}) %all-gather.2.cloned.1.call-update) | async-done | bytes 1048592 | tf_op jit(solution)/shard_map/all_gather | solution.py:204
  322.0 2.7 convolution_convert_fusion
  (200 shorter events, 57.3 us)
Async XLA Ops:
  6.5 315.4 %copy-start = (bf16[1024,512]{1,0:T(8,128)(2,1)S(1)}, bf16[1024,512]{1,0:T(8,128)(2,1)}, u32[]{:S(2)}) copy-start(bf16[1024,512]{1,0:T(8,128)(2,1)} %param.21) | copy-start | bytes 3145732
  6.5 15.7 %copy-start.21 = (bf16[128,2,8]{0,2,1:T(8,128)(2,1)S(1)}, bf16[128,2,8]{0,2,1:T(8,128)(2,1)}, u32[]{:S(2)}) copy-start(bf16[128,2,8]{0,2,1:T(8,128)(2,1)} %param.17) | copy-start | bytes 12292
  6.5 16.5 %copy-start.10 = (bf16[128,2,1024]{2,1,0:T(2,128)(2,1)S(1)}, bf16[128,2,1024]{2,1,0:T(2,128)(2,1)}, u32[]{:S(2)}) copy-start(bf16[128,2,1024]{2,1,0:T(2,128)(2,1)} %param.14) | copy-start | bytes 1572868
  6.5 18.5 %copy-start.11 = (bf16[128,2,1024]{2,1,0:T(2,128)(2,1)S(1)}, bf16[128,2,1024]{2,1,0:T(2,128)(2,1)}, u32[]{:S(2)}) copy-start(bf16[128,2,1024]{2,1,0:T(2,128)(2,1)} %param.15) | copy-start | bytes 1572868
  8.0 22.8 %all-to-all-start.1 = ((bf16[4,2,128]{2,1,0:T(2,128)(2,1)}), bf16[4,2,128]{2,1,0:T(2,128)(2,1)S(1)}, u32[]{:S(2)}, u32[]{:S(2)}) async-start(bf16[4,2,128]{2,1,0:T(2,128)(2,1)} %bitcast.131), calls=%async_computation.1 | async-start | bytes 4096 | tf_op jit(solution)/shard_map/all_to_all | solution.py:184
  12.2 14.7 %copy-start.12 = (bf16[128,1024]{1,0:T(8,128)(2,1)S(1)}, bf16[128,1024]{1,0:T(8,128)(2,1)}, u32[]{:S(2)}) copy-start(bf16[128,1024]{1,0:T(8,128)(2,1)} %param.16) | copy-start | bytes 786436
  13.5 38.7 %collective-permute-start.1 = (bf16[128,1,256]{2,0,1:T(8,128)(2,1)S(1)}, bf16[128,1,256]{2,0,1:T(8,128)(2,1)S(1)}, u32[]{:S(2)}, u32[]{:S(2)}) collective-permute-start(bf16[128,1,256]{2,0,1:T(8,128)(2,1)S(1)} %bitcast.171), channel_id=1, source_target_pairs={{0,1},{1,2},{2,3},{3,0},{4,5},{5,6},{6,7},{7,4},{8,9},{9,10},{10,1... | collective-permute-start | bytes 196616 | tf_op jit(solution)/shard_map/ppermute | solution.py:27
  14.2 38.0 %collective-permute-start.2 = (bf16[128,1,256]{2,0,1:T(8,128)(2,1)S(1)}, bf16[128,1,256]{2,0,1:T(8,128)(2,1)S(1)}, u32[]{:S(2)}, u32[]{:S(2)}) collective-permute-start(bf16[128,1,256]{2,0,1:T(8,128)(2,1)S(1)} %bitcast.172), channel_id=1, source_target_pairs={{0,2},{1,3},{2,0},{3,1},{4,6},{5,7},{6,4},{7,5},{8,10},{9,11},{10,... | collective-permute-start | bytes 196616 | tf_op jit(solution)/shard_map/ppermute | solution.py:27
  16.0 36.2 %collective-permute-start.3 = (bf16[128,1,256]{2,0,1:T(8,128)(2,1)S(1)}, bf16[128,1,256]{2,0,1:T(8,128)(2,1)S(1)}, u32[]{:S(2)}, u32[]{:S(2)}) collective-permute-start(bf16[128,1,256]{2,0,1:T(8,128)(2,1)S(1)} %bitcast.173), channel_id=1, source_target_pairs={{0,3},{1,0},{2,1},{3,2},{4,7},{5,4},{6,5},{7,6},{8,11},{9,8},{10,9... | collective-permute-start | bytes 196616 | tf_op jit(solution)/shard_map/ppermute | solution.py:27
  22.1 13.0 %copy-start.8 = (pred[8,128,128]{2,1,0:T(8,128)(4,1)}, pred[8,128,128]{2,1,0:T(8,128)(4,1)S(1)}, u32[]{:S(2)}) copy-start(pred[8,128,128]{2,1,0:T(8,128)(4,1)S(1)} %compare_and_fusion) | copy-start | bytes 393220
  30.8 7.0 %all-to-all-start.2 = ((bf16[128,2,8]{0,1,2:T(2,128)(2,1)}), bf16[128,2,8]{0,1,2:T(2,128)(2,1)S(1)}, u32[]{:S(2)}, u32[]{:S(2)}) async-start(bf16[128,2,8]{0,1,2:T(2,128)(2,1)} %copy.219), calls=%async_computation.2 | async-start | bytes 8192 | tf_op jit(solution)/shard_map/all_to_all | solution.py:183
  37.8 9.4 %all-to-all-start.4 = ((bf16[4,2,16384]{2,1,0:T(2,128)(2,1)}), bf16[4,2,16384]{2,1,0:T(2,128)(2,1)S(1)}, u32[]{:S(2)}, u32[]{:S(2)}) async-start(bf16[4,2,16384]{2,1,0:T(2,128)(2,1)} %reshape.256), calls=%async_computation.4 | async-start | bytes 524288 | tf_op jit(solution)/shard_map/all_to_all | solution.py:182
  41.7 12.7 %copy-start.13 = (f32[2,8,128]{2,1,0:T(8,128)}, f32[2,8,128]{2,1,0:T(8,128)S(1)}, u32[]{:S(2)}) copy-start(f32[2,8,128]{2,1,0:T(8,128)S(1)} %reshape.223) | copy-start | bytes 24580
  47.2 12.3 %all-to-all-start = ((bf16[128,2,1024]{0,1,2:T(2,128)(2,1)}), bf16[128,2,1024]{0,1,2:T(2,128)(2,1)S(1)}, u32[]{:S(2)}, u32[]{:S(2)}) async-start(bf16[128,2,1024]{0,1,2:T(2,128)(2,1)} %copy.211), calls=%async_computation | async-start | bytes 1048576 | tf_op jit(solution)/shard_map/all_to_all | solution.py:180
  59.5 13.1 %all-to-all-start.3 = ((bf16[128,2,1024]{0,1,2:T(2,128)(2,1)}), bf16[128,2,1024]{0,1,2:T(2,128)(2,1)}, u32[]{:S(2)}, u32[]{:S(2)}) async-start(bf16[128,2,1024]{0,1,2:T(2,128)(2,1)} %copy.221), calls=%async_computation.3 | async-start | bytes 1048576 | tf_op jit(solution)/shard_map/all_to_all | solution.py:181
  63.6 258.3 %all-gather.2.cloned.1.call-start = ((), (), s32[]{:S(2)}) async-start(), calls=%async_computation.5 | async-start | bytes 1310720 | tf_op jit(solution)/shard_map/all_gather | solution.py:204
  74.0 3.6 %copy-start.6 = (f32[128,128]{1,0:T(8,128)S(1)}, f32[128,128]{1,0:T(8,128)}, u32[]{:S(2)}) copy-start(f32[128,128]{1,0:T(8,128)} %get-tuple-element.200) | copy-start | bytes 196612
  74.0 3.6 %copy-start.14 = (f32[2,8,128]{2,1,0:T(8,128)S(1)}, f32[2,8,128]{2,1,0:T(8,128)}, u32[]{:S(2)}) copy-start(f32[2,8,128]{2,1,0:T(8,128)} %copy-done.13) | copy-start | bytes 24580
  74.0 3.6 %copy-start.18 = (pred[128,128]{1,0:T(8,128)(4,1)S(1)}, pred[128,128]{1,0:T(8,128)(4,1)}, u32[]{:S(2)}) copy-start(pred[128,128]{1,0:T(8,128)(4,1)} %get-tuple-element.198) | copy-start | bytes 49156
  74.0 3.6 %copy-start.19 = (pred[128,128]{1,0:T(8,128)(4,1)S(1)}, pred[128,128]{1,0:T(8,128)(4,1)}, u32[]{:S(2)}) copy-start(pred[128,128]{1,0:T(8,128)(4,1)} %get-tuple-element.199) | copy-start | bytes 49156
  75.5 2.1 copy-start.9
  75.5 2.1 copy-start.15
  81.1 160.9 %copy-start.17 = (f32[2,8,128]{2,1,0:T(8,128)S(1)}, f32[2,8,128]{2,1,0:T(8,128)}, u32[]{:S(2)}) copy-start(f32[2,8,128]{2,1,0:T(8,128)} %get-tuple-element.189) | copy-start | bytes 24580
  249.1 3.2 copy-start.7
  249.1 3.2 copy-start.20
  278.7 5.8 %collective-permute-start = (bf16[2,128,128]{2,1,0:T(8,128)(2,1)S(1)}, bf16[2,128,128]{2,1,0:T(8,128)(2,1)S(1)}, u32[]{:S(2)}, u32[]{:S(2)}) collective-permute-start(bf16[2,128,128]{2,1,0:T(8,128)(2,1)S(1)} %fusion.77), channel_id=1, source_target_pairs={{0,4},{4,8},{8,12},{1,5},{5,9},{9,13},{2,6},{6,10},{10,14},{3,7},{... | collective-permute-start | bytes 196616 | tf_op jit(solution)/shard_map/while/body/eval_jaxpr/ppermute | solution.py:35
  284.8 6.2 %collective-permute-start = (bf16[2,128,128]{2,1,0:T(8,128)(2,1)S(1)}, bf16[2,128,128]{2,1,0:T(8,128)(2,1)S(1)}, u32[]{:S(2)}, u32[]{:S(2)}) collective-permute-start(bf16[2,128,128]{2,1,0:T(8,128)(2,1)S(1)} %fusion.77), channel_id=1, source_target_pairs={{0,4},{4,8},{8,12},{1,5},{5,9},{9,13},{2,6},{6,10},{10,14},{3,7},{... | collective-permute-start | bytes 196616 | tf_op jit(solution)/shard_map/while/body/eval_jaxpr/ppermute | solution.py:35
  291.3 6.2 %collective-permute-start = (bf16[2,128,128]{2,1,0:T(8,128)(2,1)S(1)}, bf16[2,128,128]{2,1,0:T(8,128)(2,1)S(1)}, u32[]{:S(2)}, u32[]{:S(2)}) collective-permute-start(bf16[2,128,128]{2,1,0:T(8,128)(2,1)S(1)} %fusion.77), channel_id=1, source_target_pairs={{0,4},{4,8},{8,12},{1,5},{5,9},{9,13},{2,6},{6,10},{10,14},{3,7},{... | collective-permute-start | bytes 196616 | tf_op jit(solution)/shard_map/while/body/eval_jaxpr/ppermute | solution.py:35
  297.7 2.7 copy-start.3
  297.7 2.7 copy-start.4
  300.5 2.4 copy-start.2
  300.5 2.4 copy-start.22
  (3 other events, 5.1 us)
Sparse Core Ops, SparseCore 0:
  304.1 17.8 all-gather.1
